TPU v7x, 32 devices: a whole 2x2x4 slice. The times are simulated.
32 devices in a mesh: lat: 16 (over z, x, core), lon: 2 (over y).
Axes of the slice: x: 2, y: 2, z: 4, core: 2. Of those that a mesh axis runs over, the one named last changes fastest.
Arguments:
- fields: bfloat16 [2, 16, 1024, 256], P(None, 'lat', 'lon'), may hold values from -6 to 6
- norm_gain: float32 [256], replicated, may hold values from 0.1 to 1.9
- w_qkv: bfloat16 [256, 768], replicated, may hold values from -12 to 12
- w_out: bfloat16 [256, 256], replicated, may hold values from -1 to 1
- conv_weight: bfloat16 [256, 4, 4, 128], replicated, may hold values from -0.1875 to 0.1875
- conv_bias: float32 [128], replicated, may hold values from -3 to 3
Outputs:
- upsampled: bfloat16 [2, 32, 2048, 128], P(None, 'lat', 'lon')
All inputs are finite; a program needn't handle non-finite values.
Results may differ from a plain program's by a relative error of at most 0.0085.
Values may be sent and summed in bfloat16 or wider, within the bound.
A program may use at most 64 MiB of HBM per device.

v0:
```python
import jax
import jax.numpy as jnp
from jax import lax
from jax.sharding import PartitionSpec as P

HEADS = 8


def extended(block, sides, width, periodic):
    for axis, dim in sides:
        count = lax.axis_size(axis)
        forward = [(i, i + 1) for i in range(count - 1)]
        if periodic:
            forward.append((count - 1, 0))
        backward = [(target, source) for source, target in forward]
        low = lax.ppermute(
            lax.slice_in_dim(block, block.shape[dim] - width, None, axis=dim), axis, forward
        )
        high = lax.ppermute(lax.slice_in_dim(block, 0, width, axis=dim), axis, backward)
        block = jnp.concatenate([low, block, high], axis=dim)
    return block


def normalize(fields, norm_gain):
    values = fields.astype(jnp.float32)
    average = jnp.mean(values, axis=-1, keepdims=True)
    centred = values - average
    variance = jnp.mean(centred * centred, axis=-1, keepdims=True)
    return (centred * lax.rsqrt(variance + 1e-05) * norm_gain).astype(jnp.bfloat16)


def split_heads(row_block, head_count):
    seq_count, length, width = row_block.shape
    depth = width // head_count
    return (
        row_block.reshape(seq_count, length, head_count, depth)
        .transpose(0, 2, 1, 3)
        .reshape(seq_count * head_count, length, depth)
    )


def merge_heads(row_block, head_count):
    total_items, length, depth = row_block.shape
    seq_count = total_items // head_count
    return (
        row_block.reshape(seq_count, head_count, length, depth)
        .transpose(0, 2, 1, 3)
        .reshape(seq_count, length, head_count * depth)
    )


def fold_one(item_rows):
    query_one, key_one, value_one, max_old, total_old, sum_old = item_rows
    scores = jnp.dot(query_one, key_one.T, preferred_element_type=jnp.float32) * query_one.shape[
        -1
    ] ** (-0.5)
    max_new = jnp.maximum(max_old, jnp.max(scores, axis=-1))
    factor = jnp.exp(max_old - max_new)
    probs = jnp.exp(scores - max_new[:, None])
    total_new = total_old * factor + jnp.sum(probs, axis=-1)
    sum_new = sum_old * factor[:, None] + jnp.dot(
        probs.astype(jnp.bfloat16), value_one, preferred_element_type=jnp.float32
    )
    return (max_new, total_new, sum_new)


def fold_keys(running, query_heads, keys_rows, values_rows, head_count):
    max_old, total_old, sum_old = running
    return lax.map(
        fold_one,
        (
            query_heads,
            split_heads(keys_rows, head_count),
            split_heads(values_rows, head_count),
            max_old,
            total_old,
            sum_old,
        ),
    )


def tap_tile(hidden, conv_weight):
    batch_size, row_count, col_count, width = hidden.shape
    outward = conv_weight.shape[-1]
    taps = jnp.dot(
        hidden.reshape(-1, width),
        conv_weight.reshape(width, 16 * outward),
        preferred_element_type=jnp.float32,
    )
    taps = taps.reshape(batch_size, row_count, col_count, 2, 2, 2, 2, outward)
    total_tile = jnp.zeros((batch_size, row_count + 1, 2, col_count + 1, 2, outward), jnp.float32)
    for row_half in range(2):
        for col_half in range(2):
            portion = taps[:, :, :, row_half, :, col_half, :, :].transpose(0, 1, 3, 2, 4, 5)
            portion = jnp.pad(
                portion,
                (
                    (0, 0),
                    (row_half, 1 - row_half),
                    (0, 0),
                    (col_half, 1 - col_half),
                    (0, 0),
                    (0, 0),
                ),
            )
            total_tile = total_tile + portion
    return total_tile.reshape(batch_size, 2 * row_count + 2, 2 * col_count + 2, outward)


def per_device(fields, norm_gain, w_qkv, w_out, conv_weight, conv_bias):
    batch_size, rows_dev, cols_dev, width = fields.shape
    head_count = HEADS
    seq_count = batch_size * rows_dev
    normed = normalize(fields, norm_gain)
    flat_rows = normed.reshape(-1, width)
    projected = jnp.dot(flat_rows, w_qkv, preferred_element_type=jnp.float32).astype(jnp.bfloat16)
    projected = projected.reshape(seq_count, cols_dev, 3 * width)
    queries = projected[..., :width]
    keys_rows = projected[..., width : 2 * width]
    values_rows = projected[..., 2 * width :]
    query_heads = split_heads(queries, head_count)
    depth = width // head_count
    initial = (
        jnp.full((seq_count * head_count, cols_dev), -1e30, jnp.float32),
        jnp.zeros((seq_count * head_count, cols_dev), jnp.float32),
        jnp.zeros((seq_count * head_count, cols_dev, depth), jnp.float32),
    )
    final_state = fold_keys(
        initial,
        query_heads,
        lax.all_gather(keys_rows, "lon", axis=1, tiled=True),
        lax.all_gather(values_rows, "lon", axis=1, tiled=True),
        head_count,
    )
    attended = merge_heads(final_state[2] / final_state[1][..., None], head_count).astype(
        jnp.bfloat16
    )
    update = jnp.dot(
        attended.reshape(-1, width), w_out, preferred_element_type=jnp.float32
    ).reshape(fields.shape)
    hidden = (fields.astype(jnp.float32) + update).astype(jnp.bfloat16)
    tiled = tap_tile(hidden, conv_weight)
    edge_cols = jnp.concatenate([tiled[:, :, :1], tiled[:, :, -1:]], axis=2)
    from_cols = extended(edge_cols, (("lon", 2),), 1, True)
    middle = tiled[:, :, 1:-1]
    middle = middle.at[:, :, 0].add(from_cols[:, :, 0]).at[:, :, -1].add(from_cols[:, :, 3])
    edge_rows = jnp.concatenate([middle[:, :1], middle[:, -1:]], axis=1)
    from_rows = extended(edge_rows.astype(jnp.bfloat16), (("lat", 1),), 1, False).astype(
        edge_rows.dtype
    )
    result = middle[:, 1:-1]
    result = result.at[:, 0].add(from_rows[:, 0]).at[:, -1].add(from_rows[:, 3])
    return (result + conv_bias).astype(jnp.bfloat16)


def solution(mesh):
    in_specs = (P(None, "lat", "lon", None), P(), P(), P(), P(), P())
    out_specs = P(None, "lat", "lon", None)
    return jax.shard_map(
        per_device, mesh=mesh, in_specs=in_specs, out_specs=out_specs, check_vma=False
    )
```

profile of v0, /device:TPU:9, one launch (start us, length us, event | category | flops | bytes accessed | tf_op | source)
XLA Modules:
  0.0 182.4 jit_solution(2368253972272088851)
XLA Ops:
  7.9 1.4 fusion.21
  9.3 1.4 fusion.23
  15.9 19.1 %all-gather.5.cloned.1.call-done = bf16[2,1024,256]{1,2,0:T(8,128)(2,1)} async-done(((bf16[2,512,256]{1,2,0:T(8,128)(2,1)}), bf16[2,1024,256]{1,2,0:T(8,128)(2,1)}) %all-gather.5.cloned.1.call-update) | async-done | bytes 1048592 | tf_op jit(solution)/shard_map/all_gather | solution.py:132
  35.1 22.9 %all-gather.3.cloned.1.call-done = bf16[2,1024,256]{1,2,0:T(8,128)(2,1)} async-done(((bf16[2,512,256]{1,2,0:T(8,128)(2,1)}), bf16[2,1024,256]{1,2,0:T(8,128)(2,1)}) %all-gather.3.cloned.1.call-update) | async-done | bytes 1048592 | tf_op jit(solution)/shard_map/all_gather | solution.py:131
  57.9 74.6 %while.16 = (s32[]{:T(128)}, f32[16,512]{1,0:T(8,128)}, f32[16,512,32]{1,2,0:T(8,128)S(1)}, bf16[16,512,32]{1,2,0:T(8,128)(2,1)}, bf16[16,1024,32]{1,2,0:T(8,128...) while((s32[]{:T(128)}, f32[16,512]{1,0:T(8,128)}, f32[16,512,32]{1,2,0:T(8,128)S(1)}, ...), condition=%wide.region_5.6_spmd, body=%wide.region_2.5_spmd.sunk | while | flops 71321088 | bytes 6549601 | solution.py:69
  57.9 1.5 multiply_reduce_fusion.2
  59.9 1.4 fusion.43
  62.7 1.4 multiply_reduce_fusion.2
  64.6 1.4 fusion.43
  67.3 1.4 multiply_reduce_fusion.2
  69.3 1.4 fusion.43
  72.0 1.4 multiply_reduce_fusion.2
  73.9 1.4 fusion.43
  76.6 1.4 multiply_reduce_fusion.2
  78.6 1.4 fusion.43
  81.3 1.4 multiply_reduce_fusion.2
  83.2 1.4 fusion.43
  85.9 1.4 multiply_reduce_fusion.2
  87.9 1.4 fusion.43
  90.6 1.4 multiply_reduce_fusion.2
  92.5 1.4 fusion.43
  95.3 1.4 multiply_reduce_fusion.2
  97.2 1.4 fusion.43
  99.9 1.4 multiply_reduce_fusion.2
  101.9 1.4 fusion.43
  104.6 1.4 multiply_reduce_fusion.2
  106.5 1.4 fusion.43
  109.2 1.4 multiply_reduce_fusion.2
  111.2 1.4 fusion.43
  113.9 1.4 multiply_reduce_fusion.2
  115.8 1.4 fusion.43
  118.5 1.4 multiply_reduce_fusion.2
  120.5 1.4 fusion.43
  123.2 1.4 multiply_reduce_fusion.2
  125.1 1.4 fusion.43
  127.9 1.4 multiply_reduce_fusion.2
  129.8 1.4 fusion.43
  133.4 5.6 %convolution_bitcast_fusion = f32[2,1,512,2,2,2,2,128]{7,2,6,5,4,3,0,1:T(8,128)} fusion(bf16[2,2,2,2,128,256,1]{5,4,3,2,1,0,6:T(8,128)(2,1)S(1)} %bitcast.123, bf16[2,512,256]{1,2,0:T(8,128)(2,1)S(1)} %bitcast.125, bf16[2,1,512,256]{3,2,1,0:T(8,128)(2,1)S(1)} %copy-done.2, bf16[256,256]{1,0:T(8,128)(2,1)} %param.19), kind=kOutput, calls=%fused_computation.22 | convolution fusion | flops 1208745984 | bytes 10616832 | tf_op jit(solution)/shard_map/dot_general | solution.py:85
  139.0 4.0 %slice_bitcast_fusion.3 = (f32[2,1,2,512,2,128]{5,3,4,2,0,1:T(8,128)S(1)}, f32[2,1,2,512,2,128]{5,3,4,2,0,1:T(8,128)S(1)}, f32[2,1,2,512,2,128]{5,3,4,2,0,1:T(8,128)S(1)}, f32[2,1,2,512,2,128]{5,3,4,2,0,1:T(8,128)S(1)}) fusion(f32[2,1,512,2,2,2,2,128]{7,2,6,5,4,3,0,1:T(8,128)} %convolution_bitcast_fusion), kind=kLoop, calls=%fused_computation.26 | loop fusion | bytes 16777216 | tf_op jit(solution)/shard_map/transpose | solution.py:94
  143.5 2.2 %copy.60 = f32[2,2,2,513,2,128]{5,2,1,4,3,0:T(2,128)S(1)} copy(f32[2,2,2,513,2,128]{5,3,4,2,0,1:T(8,128)S(1)} %pad_add_fusion) | data formatting | bytes 8404992 | tf_op jit(solution)/shard_map/add | solution.py:106
  147.5 2.2 %copy.76 = f32[2,4,1024,128]{3,2,1,0:T(8,128)} copy(f32[2,4,1024,128]{3,1,2,0:T(4,128)S(1)} %slice.185) | data formatting | bytes 8388608
  149.8 1.4 scatter-add.14
  151.9 1.4 scatter-add.15
  153.4 2.7 %convert.6 = bf16[2,4,1024,128]{3,2,1,0:T(8,128)(2,1)S(1)} convert(f32[2,4,1024,128]{3,2,1,0:T(8,128)} %scatter-add.15) | non-fusion elementwise | flops 1048576 | bytes 6291456 | tf_op jit(solution)/shard_map/convert.2
  156.1 4.2 %collective-permute-start.2 = (bf16[2,1,1024,128]{3,2,1,0:T(8,128)(2,1)S(1)}, bf16[2,1,1024,128]{3,2,1,0:T(8,128)(2,1)S(1)}, u32[]{:S(2)}, u32[]{:S(2)}) collective-permute-start(bf16[2,1,1024,128]{3,2,1,0:T(8,128)(2,1)S(1)} %get-tuple-element.129), channel_id=1, source_target_pairs={{0,2},{2,4},{4,6},{6,8},{8,10},{10,12},{12,14},{14,16},{16,18},{18... | collective-permute-start | bytes 1572872 | tf_op jit(solution)/shard_map/ppermute | solution.py:16
  160.3 1.9 %collective-permute-start.3 = (bf16[2,1,1024,128]{3,2,1,0:T(8,128)(2,1)S(1)}, bf16[2,1,1024,128]{3,2,1,0:T(8,128)(2,1)S(1)}, u32[]{:S(2)}, u32[]{:S(2)}) collective-permute-start(bf16[2,1,1024,128]{3,2,1,0:T(8,128)(2,1)S(1)} %get-tuple-element.130), channel_id=1, source_target_pairs={{2,0},{4,2},{6,4},{8,6},{10,8},{12,10},{14,12},{16,14},{18,16},{20... | collective-permute-start | bytes 1572872 | tf_op jit(solution)/shard_map/ppermute | solution.py:19
  162.4 9.6 %collective-permute-done.2 = bf16[2,1,1024,128]{3,2,1,0:T(8,128)(2,1)S(1)} collective-permute-done((bf16[2,1,1024,128]{3,2,1,0:T(8,128)(2,1)S(1)}, bf16[2,1,1024,128]{3,2,1,0:T(8,128)(2,1)S(1)}, u32[]{:S(2)}, u32[]{:S(2)}) %collective-permute-start.2) | collective-permute-done | bytes 524320 | tf_op jit(solution)/shard_map/ppermute | solution.py:16
  172.1 1.6 collective-permute-done.3
  (107 shorter events, 42.8 us)
Async XLA Ops:
  6.5 4.1 %copy-start = (bf16[256,768]{1,0:T(8,128)(2,1)S(1)}, bf16[256,768]{1,0:T(8,128)(2,1)}, u32[]{:S(2)}) copy-start(bf16[256,768]{1,0:T(8,128)(2,1)} %param.18) | copy-start | bytes 1179652
  6.5 28.5 %all-gather.5.cloned.1.call-start = ((), (), s32[]{:S(2)}) async-start(), calls=%async_computation.1 | async-start | bytes 1572864 | tf_op jit(solution)/shard_map/all_gather | solution.py:132
  11.4 3.2 %copy-start.3 = (bf16[256,4,4,128]{3,2,1,0:T(4,128)(2,1)S(1)}, bf16[256,4,4,128]{3,2,1,0:T(4,128)(2,1)}, u32[]{:S(2)}) copy-start(bf16[256,4,4,128]{3,2,1,0:T(4,128)(2,1)} %param.20) | copy-start | bytes 3145732
  12.4 45.5 %all-gather.3.cloned.1.call-start = ((), (), s32[]{:S(2)}) async-start(), calls=%async_computation | async-start | bytes 1572864 | tf_op jit(solution)/shard_map/all_gather | solution.py:131
  15.4 42.6 %copy-start.4 = (f32[16,512,32]{1,2,0:T(8,128)S(1)}, f32[16,512,32]{1,2,0:T(8,128)}, u32[]{:S(2)}) copy-start(f32[16,512,32]{1,2,0:T(8,128)} %custom-call.1) | copy-start | bytes 3145732
  57.9 75.5 %copy-start.2 = (bf16[2,1,512,256]{3,2,1,0:T(8,128)(2,1)S(1)}, bf16[2,1,512,256]{3,2,1,0:T(8,128)(2,1)}, u32[]{:S(2)}) copy-start(bf16[2,1,512,256]{3,2,1,0:T(8,128)(2,1)} %param.16) | copy-start | bytes 1572868
  145.7 4.0 %collective-permute-start = (f32[2,4,1,128]{3,2,1,0:T(1,128)S(1)}, f32[2,4,1,128]{3,2,1,0:T(1,128)S(1)}, u32[]{:S(2)}, u32[]{:S(2)}) collective-permute-start(f32[2,4,1,128]{3,2,1,0:T(1,128)S(1)} %bitcast.132), channel_id=1, source_target_pairs={{0,1},{1,0},{2,3},{3,2},{4,5},{5,4},{6,7},{7,6},{8,9},{9,8},{10,11... | collective-permute-start | bytes 12296 | tf_op jit(solution)/shard_map/ppermute | solution.py:16
  146.1 5.1 %collective-permute-start.1 = (f32[2,4,1,128]{3,2,1,0:T(1,128)S(1)}, f32[2,4,1,128]{3,2,1,0:T(1,128)S(1)}, u32[]{:S(2)}, u32[]{:S(2)}) collective-permute-start(f32[2,4,1,128]{3,2,1,0:T(1,128)S(1)} %bitcast.131), channel_id=1, source_target_pairs={{1,0},{0,1},{3,2},{2,3},{5,4},{4,5},{7,6},{6,7},{9,8},{8,9},{11,10... | collective-permute-start | bytes 12296 | tf_op jit(solution)/shard_map/ppermute | solution.py:19
  153.4 8.9 %copy-start.1 = (f32[2,4,1024,128]{3,2,1,0:T(8,128)S(1)}, f32[2,4,1024,128]{3,2,1,0:T(8,128)}, u32[]{:S(2)}) copy-start(f32[2,4,1024,128]{3,2,1,0:T(8,128)} %scatter-add.15) | copy-start | bytes 12582916
  156.1 15.9 %collective-permute-start.2 = (bf16[2,1,1024,128]{3,2,1,0:T(8,128)(2,1)S(1)}, bf16[2,1,1024,128]{3,2,1,0:T(8,128)(2,1)S(1)}, u32[]{:S(2)}, u32[]{:S(2)}) collective-permute-start(bf16[2,1,1024,128]{3,2,1,0:T(8,128)(2,1)S(1)} %get-tuple-element.129), channel_id=1, source_target_pairs={{0,2},{2,4},{4,6},{6,8},{8,10},{10,12},{12,14},{14,16},{16,18},{18... | collective-permute-start | bytes 1572872 | tf_op jit(solution)/shard_map/ppermute | solution.py:16
  160.3 13.3 %collective-permute-start.3 = (bf16[2,1,1024,128]{3,2,1,0:T(8,128)(2,1)S(1)}, bf16[2,1,1024,128]{3,2,1,0:T(8,128)(2,1)S(1)}, u32[]{:S(2)}, u32[]{:S(2)}) collective-permute-start(bf16[2,1,1024,128]{3,2,1,0:T(8,128)(2,1)S(1)} %get-tuple-element.130), channel_id=1, source_target_pairs={{2,0},{4,2},{6,4},{8,6},{10,8},{12,10},{14,12},{16,14},{18,16},{20... | collective-permute-start | bytes 1572872 | tf_op jit(solution)/shard_map/ppermute | solution.py:19
  173.8 0.7 copy-start.5
Sparse Core Ops, SparseCore 0:
  12.5 22.4 all-gather.4
  36.6 21.2 all-gather.2
where the time goes:
time: 185 us; the launch traced here: 182 us
  waiting for transfers between devices  53.3 us (29%)
  matrix products  50.4 us (27%)
  local copies, waits for them, and re-layouts  38.1 us (21%)
  other arithmetic  19.2 us (10%)
  between operations  13.6 us (7%)
  starting transfers between devices  7.71 us (4%)
    all_gather x1, waiting for transfers between devices, per_device(): lax.all_gather(keys_rows, 'lon', axis=1, tiled=True)  22.9 us
    dot_general x16, matrix products, fold_one(): jnp.dot(query_one, key_one.T, preferred_element_type=jnp.float32)  22.4 us
    dot_general x16, matrix products, fold_one(): jnp.dot(probs.astype(jnp.bfloat16), value_one, preferred_element_type=jnp...  21.9 us
    dynamic_update_slice x16, local copies, waits for them, and re-layouts, fold_keys(): lax.map(fold_one, (query_heads, split_heads(keys_rows, head_count), split...  21.4 us
    all_gather x1, waiting for transfers between devices, per_device(): lax.all_gather(values_rows, 'lon', axis=1, tiled=True)  19.1 us
    ppermute x2, waiting for transfers between devices, extended(): lax.ppermute(lax.slice_in_dim(block, block.shape[dim] - width, None, axis...  9.64 us
    reduce_sum x16, other arithmetic, fold_one(): total_new = total_old * factor + jnp.sum(probs, axis=-1)  8.51 us
    unnamed x16, local copies, waits for them, and re-layouts  5.74 us
  transfers between devices with their start and end apart: 6, of which 4 were waited for; matrix products, arithmetic and copies ran while one was open for 4% of the time, Pallas kernels for 0%

commit v1 on v0

v1 whole, which is shorter than its diff:
```python
import functools
import math

import jax
import jax.numpy as jnp
from jax import lax
from jax.experimental import pallas as pl
from jax.experimental.pallas import tpu as pltpu
from jax.sharding import PartitionSpec as P

HEADS = 8
EDGE = 16
MESH = pl.DeviceIdType.MESH
F32 = jnp.float32
BF16 = jnp.bfloat16


def dot(a, b):
    return jnp.dot(a, b, preferred_element_type=F32)


def dot_nt(a, b):
    return lax.dot_general(a, b, (((1,), (1,)), ((), ())), preferred_element_type=F32)


def kernel(
    n_lat,
    n_lon,
    fields,
    gain,
    w_qkv,
    w_out,
    conv_w,
    bias,
    out,
    peers,
    queries,
    w_t,
    acc,
    maxima,
    att,
    hid,
    wide,
    f_send,
    f_recv,
    h_send,
    h_recv,
):
    batch, cols, width = fields.shape
    depth = width // HEADS
    outward = bias.shape[-1]
    lat = lax.axis_index("lat")
    lon = lax.axis_index("lon")
    scale = depth ** (-0.5) * math.log2(math.e)
    right = lax.rem(lon + 1, n_lon)
    left = lax.rem(lon + n_lon - 1, n_lon)
    has = {-1: lat > 0, 0: None, 1: lat < n_lat - 1}
    near = sorted({0, 1, n_lon - 1})

    def guarded(step, body):
        if has[step] is None:
            body()
        else:
            pl.when(has[step])(body)

    barrier = pltpu.get_barrier_semaphore()
    for step in (0, -1, 1):
        offsets = range(1, n_lon) if step == 0 else near

        def greet(step=step, offsets=offsets):
            for offset in offsets:
                pl.semaphore_signal(
                    barrier,
                    inc=1,
                    device_id=(lat + step, lax.rem(lon + offset, n_lon)),
                    device_id_type=MESH,
                )

        guarded(step, greet)
    sides = jnp.minimum(lat, 1) + jnp.minimum(n_lat - 1 - lat, 1)
    pl.semaphore_wait(barrier, n_lon - 1 + len(near) * sides)

    def field_copy(d, b):
        return pltpu.make_async_remote_copy(
            src_ref=fields.at[b],
            dst_ref=peers.at[d - 1, b],
            send_sem=f_send.at[d - 1, b],
            recv_sem=f_recv.at[d - 1, b],
            device_id=(lat, lax.rem(lon + d, n_lon)),
            device_id_type=MESH,
        )

    for b in range(batch):
        for d in range(1, n_lon):
            field_copy(d, b).start()

    def normalize(block):
        values = block.astype(F32)
        centred = values - jnp.mean(values, axis=-1, keepdims=True)
        variance = jnp.mean(centred * centred, axis=-1, keepdims=True)
        return (centred * lax.rsqrt(variance + 1e-05) * gain[...]).astype(BF16)

    w_t[0] = w_qkv[:, :width].T
    w_t[1] = w_qkv[:, 2 * width :].T

    for step, slot in ((-1, 0), (1, 2)):

        @pl.when(jnp.logical_not(has[step]))
        def _(slot=slot):
            hid[slot] = jnp.zeros_like(hid[slot])

    def attend(b, normed, first):
        keys = dot(normed, w_qkv[:, width : 2 * width]).astype(BF16)
        values_t = dot_nt(w_t[1], normed).astype(BF16)
        ones = jnp.ones((16, cols), BF16)
        for h in range(HEADS):
            rows = slice(h * depth, (h + 1) * depth)
            scores = dot(keys[:, rows], queries[b, rows, :])
            top = jnp.max(scores, axis=0, keepdims=True)
            if not first:
                old = maxima[b, h, 0:1, :]
                top = jnp.maximum(top, old)
                factor = jnp.exp2((old - top) * scale)
            maxima[b, h, 0:1, :] = top
            probs = jnp.exp2((scores - top) * scale).astype(BF16)
            summed = dot(jnp.concatenate([values_t[rows], ones], axis=0), probs)
            if first:
                acc[b, h] = summed
            else:
                acc[b, h] = acc[b, h] * factor + summed

    def local_block(b, carry):
        normed = normalize(fields[b])
        queries[b] = dot_nt(w_t[0], normed).astype(BF16)
        attend(b, normed, True)
        return carry

    lax.fori_loop(0, batch, local_block, 0)

    core = slice(EDGE, EDGE + cols)

    def halo(step, part, b):
        if part == 0:
            source, target, column = core, core, lon
        elif part == 1:
            source, target, column = slice(cols, EDGE + cols), slice(0, EDGE), right
        else:
            source, target, column = (
                slice(EDGE, 2 * EDGE),
                slice(EDGE + cols, 2 * EDGE + cols),
                left,
            )
        index = (step + 1) * 3 + part
        return pltpu.make_async_remote_copy(
            src_ref=hid.at[1, b, source],
            dst_ref=hid.at[1 - step, b, target],
            send_sem=h_send.at[b, index],
            recv_sem=h_recv.at[b, index],
            device_id=(lat + step, column),
            device_id_type=MESH,
        )

    parts = {-1: (0, 1, 2), 0: (1, 2), 1: (0, 1, 2)}

    def finish(b):
        for h in range(HEADS):
            att[h * depth : (h + 1) * depth, :] = (
                acc[b, h, :depth, :] / acc[b, h, depth : depth + 1, :]
            ).astype(BF16)
        update = dot(att[...].T, w_out[...])
        hid[1, b, core] = (fields[b].astype(F32) + update).astype(BF16)
        for step in (-1, 1, 0):

            def send(step=step):
                for part in parts[step]:
                    halo(step, part, b).start()

            guarded(step, send)

    for d in range(1, n_lon):

        def remote_block(b, carry, d=d):
            field_copy(d, b).wait_recv()
            attend(b, normalize(peers[d - 1, b]), False)
            if d == n_lon - 1:
                finish(b)
            return carry

        lax.fori_loop(0, batch, remote_block, 0)

    def upsample(b, carry):
        for step in (0, -1, 1):

            def arrive(step=step):
                for part in parts[step]:
                    halo(step, part, b).wait_recv()

            guarded(-step, arrive)
        for p in range(2):
            own, other = 1 + p, 3 * (1 - p)
            taps = dot(hid[1, b], conv_w[:, own * 4 * outward : (own + 1) * 4 * outward])
            taps = taps + dot(
                hid[2 * p, b], conv_w[:, other * 4 * outward : (other + 1) * 4 * outward]
            )
            even = (
                taps[EDGE : EDGE + cols, outward : 2 * outward]
                + taps[EDGE - 1 : EDGE - 1 + cols, 3 * outward :]
            )
            odd = (
                taps[EDGE : EDGE + cols, 2 * outward : 3 * outward]
                + taps[EDGE + 1 : EDGE + 1 + cols, :outward]
            )
            wide[pl.ds(0, cols, stride=2), :] = even + bias[...]
            wide[pl.ds(1, cols, stride=2), :] = odd + bias[...]
            out[b, p] = wide[...].astype(BF16)
        return carry

    lax.fori_loop(0, batch, upsample, 0)

    for b in range(batch):
        for d in range(1, n_lon):
            field_copy(d, b).wait_send()
        for step in (-1, 0, 1):

            def sent(step=step, b=b):
                for part in parts[step]:
                    halo(step, part, b).wait_send()

            guarded(step, sent)


def per_device(n_lat, n_lon, fields, norm_gain, w_qkv, w_out, conv_weight, conv_bias):
    batch, rows, cols, width = fields.shape
    assert rows == 1
    outward = conv_weight.shape[-1]
    depth = width // HEADS
    vmem = pl.BlockSpec(memory_space=pltpu.VMEM)
    return pl.pallas_call(
        functools.partial(kernel, n_lat, n_lon),
        out_shape=jax.ShapeDtypeStruct((batch, 2, 2 * cols, outward), BF16),
        in_specs=[vmem] * 6,
        out_specs=vmem,
        scratch_shapes=[
            pltpu.VMEM((n_lon - 1, batch, cols, width), BF16),
            pltpu.VMEM((batch, width, cols), BF16),
            pltpu.VMEM((2, width, width), BF16),
            pltpu.VMEM((batch, HEADS, depth + 16, cols), F32),
            pltpu.VMEM((batch, HEADS, 8, cols), F32),
            pltpu.VMEM((width, cols), BF16),
            pltpu.VMEM((3, batch, cols + 2 * EDGE, width), BF16),
            pltpu.VMEM((2 * cols, outward), F32),
            pltpu.SemaphoreType.DMA((n_lon - 1, batch)),
            pltpu.SemaphoreType.DMA((n_lon - 1, batch)),
            pltpu.SemaphoreType.DMA((batch, 9)),
            pltpu.SemaphoreType.DMA((batch, 9)),
        ],
        compiler_params=pltpu.CompilerParams(
            collective_id=0, has_side_effects=True, vmem_limit_bytes=48 * 1024 * 1024
        ),
        name="axial",
    )(
        fields.reshape(batch, cols, width),
        norm_gain.reshape(1, width),
        w_qkv,
        w_out,
        conv_weight.reshape(width, 16 * outward),
        conv_bias.reshape(1, outward),
    )


def solution(mesh):
    in_specs = (P(None, "lat", "lon", None), P(), P(), P(), P(), P())
    out_specs = P(None, "lat", "lon", None)
    return jax.shard_map(
        functools.partial(per_device, mesh.shape["lat"], mesh.shape["lon"]),
        mesh=mesh,
        in_specs=in_specs,
        out_specs=out_specs,
        check_vma=False,
    )
```

time: 185 us -> 33.7 us (0.18); the launches traced: 182 us -> 33.5 us
  waiting for transfers between devices: 53.3 us -> 0 us
  matrix products: 50.4 us -> 0 us
  local copies, waits for them, and re-layouts: 38.1 us -> 2.91 us
  Pallas kernels: 0 us -> 30.6 us
  other arithmetic: 19.2 us -> 0 us
  between operations: 13.6 us -> 0.08 us
  starting transfers between devices: 7.71 us -> 0 us
    dot_general x34 -> x0, matrix products: 50.4 us -> none  [the longest x16 22.4 us: fold_one(): jnp.dot(query_one, key_one.T, preferred_element_type=jnp.float32)]
    all_gather x2 -> x0, waiting for transfers between devices: 42 us -> none  [the longest x1 22.9 us: per_device(): lax.all_gather(keys_rows, 'lon', axis=1, tiled=True)]
    pallas_call x0 -> x1, Pallas kernels: none -> 30.6 us  [per_device(): pl.pallas_call(functools.partial(kernel, n_lat, n_lon), out_shape=jax.Sha...]
    dynamic_update_slice x16 -> x0, local copies, waits for them, and re-layouts: 21.4 us -> none  [fold_keys(): lax.map(fold_one, (query_heads, split_heads(keys_rows, head_count), split...]
    ppermute x4 -> x0, waiting for transfers between devices: 11.3 us -> none  [the longest x2 9.64 us: extended(): lax.ppermute(lax.slice_in_dim(block, block.shape[dim] - width, None, axis...]
    reduce_sum x18 -> x0, other arithmetic: 11.2 us -> none  [the longest x16 8.51 us: fold_one(): total_new = total_old * factor + jnp.sum(probs, axis=-1)]
    ppermute x4 -> x0, starting transfers between devices: 7.67 us -> none  [the longest x2 4.55 us: extended(): lax.ppermute(lax.slice_in_dim(block, block.shape[dim] - width, None, axis...]
    unnamed x16 -> x11, local copies, waits for them, and re-layouts: 5.74 us -> 0.99 us
  transfers between devices with their start and end apart: 6 -> 0, of which waited for: 4 -> 0; matrix products, arithmetic and copies ran while one was open for 4% -> 0% of each run, Pallas kernels for 0% -> 0%
where the time goes in v1:
time: 33.7 us; the launch traced here: 33.5 us
  Pallas kernels  30.6 us (91%)
  local copies, waits for them, and re-layouts  2.91 us (9%)
    pallas_call x1, Pallas kernels, per_device(): pl.pallas_call(functools.partial(kernel, n_lat, n_lon), out_shape=jax.Sha...  30.6 us
    reshape x1, local copies, waits for them, and re-layouts, per_device(): conv_weight.reshape(width, 16 * outward)  1.92 us
    unnamed x11, local copies, waits for them, and re-layouts  0.99 us

profile of v1, /device:TPU:9, one launch (start us, length us, event | category | flops | bytes accessed | tf_op | source)
XLA Modules:
  0.0 33.5 jit_solution(13344309007772793752)
XLA Ops:
  0.0 0.0 copy-start
  0.0 0.0 copy-start.1
  0.0 0.0 copy-start.2
  0.0 0.0 copy-start.3
  0.0 0.0 copy-start.4
  0.0 1.9 %reshape.14.conv_w = bf16[256,2048]{1,0:T(8,128)(2,1)S(1)} reshape(bf16[256,4,4,128]{3,2,1,0:T(4,128)(2,1)} %param.10) | data formatting | bytes 2097152 | tf_op jit(solution)/shard_map/reshape | solution.py:266
  2.0 0.0 copy-done
  2.0 0.0 copy-done.1
  2.0 0.0 copy-done.2
  2.0 0.0 copy-done.3
  2.0 0.0 copy-done.4
  2.0 30.6 %axial.1 = bf16[2,2,1024,128]{3,2,1,0:T(8,128)(2,1)S(1)} custom-call(bf16[2,512,256]{2,1,0:T(8,128)(2,1)S(1)} %bitcast.3, f32[1,256]{1,0:T(1,128)S(1)} %bitcast.4, bf16[256,768]{1,0:T(8,128)(2,1)S(1)} %copy-done.1, bf16[256,256]{1,0:T(8,128)(2,1)S(1)} %copy-done.2, bf16[256,2048]{1,0:T(8,128)(2,1)S(1)} %reshape.14.conv_w, f32[1,128]{1,0:T(1,128)S(1)} %bitcast.5), custom_call_target="tpu_custom_call" | custom-call | tf_op jit(solution)/shard_map/axial/pallas_call | solution.py:238
  32.6 1.0 %copy.8 = bf16[2,2,1024,128]{3,2,1,0:T(8,128)(2,1)} copy(bf16[2,2,1024,128]{3,2,1,0:T(8,128)(2,1)S(1)} %axial.1) | data formatting | bytes 2097152
Async XLA Ops:
  0.0 2.0 %copy-start = (bf16[2,1,512,256]{3,2,1,0:T(8,128)(2,1)S(1)}, bf16[2,1,512,256]{3,2,1,0:T(8,128)(2,1)}, u32[]{:S(2)}) copy-start(bf16[2,1,512,256]{3,2,1,0:T(8,128)(2,1)} %param.6) | copy-start | bytes 1572868
  0.0 2.0 %copy-start.1 = (bf16[256,768]{1,0:T(8,128)(2,1)S(1)}, bf16[256,768]{1,0:T(8,128)(2,1)}, u32[]{:S(2)}) copy-start(bf16[256,768]{1,0:T(8,128)(2,1)} %w_qkv.1) | copy-start | bytes 1179652
  0.0 2.0 %copy-start.2 = (bf16[256,256]{1,0:T(8,128)(2,1)S(1)}, bf16[256,256]{1,0:T(8,128)(2,1)}, u32[]{:S(2)}) copy-start(bf16[256,256]{1,0:T(8,128)(2,1)} %w_out.1) | copy-start | bytes 393220
  0.0 2.0 %copy-start.3 = (f32[256]{0:T(256)S(1)}, f32[256]{0:T(256)}, u32[]{:S(2)}) copy-start(f32[256]{0:T(256)} %param.7) | copy-start | bytes 3076
  0.0 2.0 %copy-start.4 = (f32[128]{0:T(128)S(1)}, f32[128]{0:T(128)}, u32[]{:S(2)}) copy-start(f32[128]{0:T(128)} %param.11) | copy-start | bytes 1540

commit v2 on v1

--- a/solution.py
+++ b/solution.py
@@ -10,6 +10,8 @@
 
 HEADS = 8
 EDGE = 16
+GROUP = 128
+CHUNKS = 2
 MESH = pl.DeviceIdType.MESH
 F32 = jnp.float32
 BF16 = jnp.bfloat16
@@ -35,10 +37,9 @@
     out,
     peers,
     queries,
-    w_t,
     acc,
+    totals,
     maxima,
-    att,
     hid,
     wide,
     f_send,
@@ -48,6 +49,7 @@
 ):
     batch, cols, width = fields.shape
     depth = width // HEADS
+    chunk = cols // CHUNKS
     outward = bias.shape[-1]
     lat = lax.axis_index("lat")
     lon = lax.axis_index("lon")
@@ -100,57 +102,77 @@
         variance = jnp.mean(centred * centred, axis=-1, keepdims=True)
         return (centred * lax.rsqrt(variance + 1e-05) * gain[...]).astype(BF16)
 
-    w_t[0] = w_qkv[:, :width].T
-    w_t[1] = w_qkv[:, 2 * width :].T
-
     for step, slot in ((-1, 0), (1, 2)):
 
         @pl.when(jnp.logical_not(has[step]))
         def _(slot=slot):
             hid[slot] = jnp.zeros_like(hid[slot])
 
-    def attend(b, normed, first):
+    head = lax.broadcasted_iota(jnp.int32, (chunk, GROUP), 1) // depth
+    per_group = GROUP // depth
+
+    def project(b, block, with_queries):
+        normed = normalize(block)
+        if with_queries:
+            queries[b] = dot(normed, w_qkv[:, :width]).astype(BF16)
         keys = dot(normed, w_qkv[:, width : 2 * width]).astype(BF16)
-        values_t = dot_nt(w_t[1], normed).astype(BF16)
-        ones = jnp.ones((16, cols), BF16)
-        for h in range(HEADS):
-            rows = slice(h * depth, (h + 1) * depth)
-            scores = dot(keys[:, rows], queries[b, rows, :])
-            top = jnp.max(scores, axis=0, keepdims=True)
+        return keys, dot(normed, w_qkv[:, 2 * width :]).astype(BF16)
+
+    def attend(b, c, keys, values, first):
+        rows = slice(c * chunk, (c + 1) * chunk)
+        for g in range(width // GROUP):
+            lanes = slice(g * GROUP, (g + 1) * GROUP)
+            query = queries[b, rows, lanes]
+            stacked = jnp.concatenate(
+                [query * (head == h).astype(BF16) for h in range(per_group)], axis=0
+            )
+            scores = dot_nt(stacked, keys[:, lanes])
+            top = jnp.max(scores, axis=-1, keepdims=True)
+            probs = jnp.exp2((scores - top) * scale).astype(BF16)
+            ones = jnp.ones((cols, GROUP), BF16)
+            mixed = dot(probs, jnp.concatenate([values[:, lanes], ones], axis=1))
+
+            def merge(stack):
+                merged = jnp.broadcast_to(stack[:chunk], (chunk, GROUP))
+                for h in range(1, per_group):
+                    merged = jnp.where(head == h, stack[h * chunk : (h + 1) * chunk], merged)
+                return merged
+
+            new_sum, new_total, new_top = (
+                merge(mixed[:, :GROUP]),
+                merge(mixed[:, GROUP:]),
+                merge(top),
+            )
             if not first:
-                old = maxima[b, h, 0:1, :]
-                top = jnp.maximum(top, old)
-                factor = jnp.exp2((old - top) * scale)
-            maxima[b, h, 0:1, :] = top
-            probs = jnp.exp2((scores - top) * scale).astype(BF16)
-            summed = dot(jnp.concatenate([values_t[rows], ones], axis=0), probs)
-            if first:
-                acc[b, h] = summed
-            else:
-                acc[b, h] = acc[b, h] * factor + summed
+                old_top = maxima[b, rows, lanes]
+                both = jnp.maximum(old_top, new_top)
+                old_factor = jnp.exp2((old_top - both) * scale)
+                new_factor = jnp.exp2((new_top - both) * scale)
+                new_sum = acc[b, rows, lanes] * old_factor + new_sum * new_factor
+                new_total = totals[b, rows, lanes] * old_factor + new_total * new_factor
+                new_top = both
+            acc[b, rows, lanes] = new_sum
+            totals[b, rows, lanes] = new_total
+            maxima[b, rows, lanes] = new_top
 
     def local_block(b, carry):
-        normed = normalize(fields[b])
-        queries[b] = dot_nt(w_t[0], normed).astype(BF16)
-        attend(b, normed, True)
+        keys, values = project(b, fields[b], True)
+        for c in range(CHUNKS):
+            attend(b, c, keys, values, True)
         return carry
 
     lax.fori_loop(0, batch, local_block, 0)
 
-    core = slice(EDGE, EDGE + cols)
-
     def halo(step, part, b):
-        if part == 0:
-            source, target, column = core, core, lon
-        elif part == 1:
+        if part < CHUNKS:
+            source = target = slice(EDGE + part * chunk, EDGE + (part + 1) * chunk)
+            column = lon
+        elif part == CHUNKS:
+            source, target = slice(EDGE, 2 * EDGE), slice(EDGE + cols, 2 * EDGE + cols)
+            column = left
+        else:
             source, target, column = slice(cols, EDGE + cols), slice(0, EDGE), right
-        else:
-            source, target, column = (
-                slice(EDGE, 2 * EDGE),
-                slice(EDGE + cols, 2 * EDGE + cols),
-                left,
-            )
-        index = (step + 1) * 3 + part
+        index = (step + 1) * (CHUNKS + 2) + part
         return pltpu.make_async_remote_copy(
             src_ref=hid.at[1, b, source],
             dst_ref=hid.at[1 - step, b, target],
@@ -160,20 +182,27 @@
             device_id_type=MESH,
         )
 
-    parts = {-1: (0, 1, 2), 0: (1, 2), 1: (0, 1, 2)}
-
-    def finish(b):
-        for h in range(HEADS):
-            att[h * depth : (h + 1) * depth, :] = (
-                acc[b, h, :depth, :] / acc[b, h, depth : depth + 1, :]
-            ).astype(BF16)
-        update = dot(att[...].T, w_out[...])
-        hid[1, b, core] = (fields[b].astype(F32) + update).astype(BF16)
+    edges = (CHUNKS, CHUNKS + 1)
+    parts = {-1: (*range(CHUNKS), *edges), 0: edges, 1: (*range(CHUNKS), *edges)}
+
+    def finish(b, c):
+        rows = slice(c * chunk, (c + 1) * chunk)
+        attended = (acc[b, rows] / totals[b, rows]).astype(BF16)
+        update = dot(attended, w_out[...])
+        hid[1, b, EDGE + c * chunk : EDGE + (c + 1) * chunk] = (
+            fields[b, rows].astype(F32) + update
+        ).astype(BF16)
+        ready = [c]
+        if c == 0:
+            ready.append(CHUNKS)
+        if c == CHUNKS - 1:
+            ready.append(CHUNKS + 1)
         for step in (-1, 1, 0):
 
             def send(step=step):
-                for part in parts[step]:
-                    halo(step, part, b).start()
+                for part in ready:
+                    if part in parts[step]:
+                        halo(step, part, b).start()
 
             guarded(step, send)
 
@@ -181,9 +210,11 @@
 
         def remote_block(b, carry, d=d):
             field_copy(d, b).wait_recv()
-            attend(b, normalize(peers[d - 1, b]), False)
-            if d == n_lon - 1:
-                finish(b)
+            keys, values = project(b, peers[d - 1, b], False)
+            for c in range(CHUNKS):
+                attend(b, c, keys, values, False)
+                if d == n_lon - 1:
+                    finish(b, c)
             return carry
 
         lax.fori_loop(0, batch, remote_block, 0)
@@ -233,7 +264,6 @@
     batch, rows, cols, width = fields.shape
     assert rows == 1
     outward = conv_weight.shape[-1]
-    depth = width // HEADS
     vmem = pl.BlockSpec(memory_space=pltpu.VMEM)
     return pl.pallas_call(
         functools.partial(kernel, n_lat, n_lon),
@@ -242,17 +272,16 @@
         out_specs=vmem,
         scratch_shapes=[
             pltpu.VMEM((n_lon - 1, batch, cols, width), BF16),
-            pltpu.VMEM((batch, width, cols), BF16),
-            pltpu.VMEM((2, width, width), BF16),
-            pltpu.VMEM((batch, HEADS, depth + 16, cols), F32),
-            pltpu.VMEM((batch, HEADS, 8, cols), F32),
-            pltpu.VMEM((width, cols), BF16),
+            pltpu.VMEM((batch, cols, width), BF16),
+            pltpu.VMEM((batch, cols, width), F32),
+            pltpu.VMEM((batch, cols, width), F32),
+            pltpu.VMEM((batch, cols, width), F32),
             pltpu.VMEM((3, batch, cols + 2 * EDGE, width), BF16),
             pltpu.VMEM((2 * cols, outward), F32),
             pltpu.SemaphoreType.DMA((n_lon - 1, batch)),
             pltpu.SemaphoreType.DMA((n_lon - 1, batch)),
-            pltpu.SemaphoreType.DMA((batch, 9)),
-            pltpu.SemaphoreType.DMA((batch, 9)),
+            pltpu.SemaphoreType.DMA((batch, 3 * (CHUNKS + 2))),
+            pltpu.SemaphoreType.DMA((batch, 3 * (CHUNKS + 2))),
         ],
         compiler_params=pltpu.CompilerParams(
             collective_id=0, has_side_effects=True, vmem_limit_bytes=48 * 1024 * 1024

time: 33.7 us -> 31.6 us (0.938)
  Pallas kernels: 30.6 us -> 28.5 us
    pallas_call x1, Pallas kernels: 30.6 us -> 28.5 us  [per_device(): pl.pallas_call(functools.partial(kernel, n_lat, n_lon), out_shape=jax.Sha...]
where the time goes in v2:
time: 31.6 us; the launch traced here: 31.5 us
  Pallas kernels  28.5 us (90%)
  local copies, waits for them, and re-layouts  2.91 us (9%)
    pallas_call x1, Pallas kernels, per_device(): pl.pallas_call(functools.partial(kernel, n_lat, n_lon), out_shape=jax.Sha...  28.5 us
    reshape x1, local copies, waits for them, and re-layouts, per_device(): conv_weight.reshape(width, 16 * outward)  1.92 us
    unnamed x11, local copies, waits for them, and re-layouts  0.99 us

profile of v2, /device:TPU:9, one launch (start us, length us, event | category | flops | bytes accessed | tf_op | source)
XLA Modules:
  0.0 31.5 jit_solution(112173364963897388)
XLA Ops:
  0.0 0.0 copy-start
  0.0 0.0 copy-start.1
  0.0 0.0 copy-start.2
  0.0 0.0 copy-start.3
  0.0 0.0 copy-start.4
  0.0 1.9 %reshape.14.conv_w = bf16[256,2048]{1,0:T(8,128)(2,1)S(1)} reshape(bf16[256,4,4,128]{3,2,1,0:T(4,128)(2,1)} %param.10) | data formatting | bytes 2097152 | tf_op jit(solution)/shard_map/reshape | solution.py:295
  2.0 0.0 copy-done
  2.0 0.0 copy-done.1
  2.0 0.0 copy-done.2
  2.0 0.0 copy-done.3
  2.0 0.0 copy-done.4
  2.0 28.5 %axial.1 = bf16[2,2,1024,128]{3,2,1,0:T(8,128)(2,1)S(1)} custom-call(bf16[2,512,256]{2,1,0:T(8,128)(2,1)S(1)} %bitcast.3, f32[1,256]{1,0:T(1,128)S(1)} %bitcast.4, bf16[256,768]{1,0:T(8,128)(2,1)S(1)} %copy-done.1, bf16[256,256]{1,0:T(8,128)(2,1)S(1)} %copy-done.2, bf16[256,2048]{1,0:T(8,128)(2,1)S(1)} %reshape.14.conv_w, f32[1,128]{1,0:T(1,128)S(1)} %bitcast.5), custom_call_target="tpu_custom_call" | custom-call | tf_op jit(solution)/shard_map/axial/pallas_call | solution.py:268
  30.5 1.0 %copy.8 = bf16[2,2,1024,128]{3,2,1,0:T(8,128)(2,1)} copy(bf16[2,2,1024,128]{3,2,1,0:T(8,128)(2,1)S(1)} %axial.1) | data formatting | bytes 2097152
Async XLA Ops:
  0.0 2.0 %copy-start = (bf16[2,1,512,256]{3,2,1,0:T(8,128)(2,1)S(1)}, bf16[2,1,512,256]{3,2,1,0:T(8,128)(2,1)}, u32[]{:S(2)}) copy-start(bf16[2,1,512,256]{3,2,1,0:T(8,128)(2,1)} %param.6) | copy-start | bytes 1572868
  0.0 2.0 %copy-start.1 = (bf16[256,768]{1,0:T(8,128)(2,1)S(1)}, bf16[256,768]{1,0:T(8,128)(2,1)}, u32[]{:S(2)}) copy-start(bf16[256,768]{1,0:T(8,128)(2,1)} %w_qkv.1) | copy-start | bytes 1179652
  0.0 2.0 %copy-start.2 = (bf16[256,256]{1,0:T(8,128)(2,1)S(1)}, bf16[256,256]{1,0:T(8,128)(2,1)}, u32[]{:S(2)}) copy-start(bf16[256,256]{1,0:T(8,128)(2,1)} %w_out.1) | copy-start | bytes 393220
  0.0 2.0 %copy-start.3 = (f32[256]{0:T(256)S(1)}, f32[256]{0:T(256)}, u32[]{:S(2)}) copy-start(f32[256]{0:T(256)} %param.7) | copy-start | bytes 3076
  0.0 2.0 %copy-start.4 = (f32[128]{0:T(128)S(1)}, f32[128]{0:T(128)}, u32[]{:S(2)}) copy-start(f32[128]{0:T(128)} %param.11) | copy-start | bytes 1540
